TPU v7x, 256 devices: a whole 4x4x8 slice. The times are simulated.
256 devices in a mesh: expert: 8 (over x, core), tensor: 32 (over y, z).
Axes of the slice: x: 4, y: 4, z: 8, core: 2. Of those that a mesh axis runs over, the one named last changes fastest.
Arguments:
- tokens: bfloat16 [1024, 6144], P('expert'), may hold values from -6 to 6
- routes: int32 [1024, 2], P('expert'), may hold values from 0 to 7, all different within a row; in each aligned block of 128 rows (0 to 127, 128 to 255, ...) at most 64 rows name the same one
- gate_num: int32 [1024, 2], P('expert'), may hold values from 1 to 15
- gate_weight: bfloat16 [8, 6144, 8192], P('expert', None, 'tensor'), may hold values from -0.078125 to 0.078125
- up_weight: bfloat16 [8, 6144, 8192], P('expert', None, 'tensor'), may hold values from -0.078125 to 0.078125
- down_weight: bfloat16 [8, 8192, 6144], P('expert', 'tensor'), may hold values from -0.125 to 0.125
Outputs:
- mixed: bfloat16 [1024, 6144], P('expert', 'tensor')
Inputs may be any that keep to these rules, and one draw needn't show every extreme that they name: `routes`: within the 128 tokens of one index of expert, the two experts of a token differ, no expert is named by more than 64 tokens, a bound that some block reaches.
All inputs are finite; a program needn't handle non-finite values.
Results may differ from a plain program's by a relative error of at most 0.027.
Values may be sent and summed in bfloat16 or wider, within the bound.
A program may use at most 64 MiB of HBM per device.

v0:
```python
import math

import jax
import jax.numpy as jnp
from jax import lax
from jax.sharding import PartitionSpec as P

CAP = 64


denominator = 16.0


def partner_2(value, axis, apart):
    return lax.ppermute(value, axis, [(i, i ^ 1 << apart) for i in range(lax.axis_size(axis))])


def slot_tables(route_block, numer_block, expert_count):
    chosen = route_block.reshape(-1)
    expert_row = jnp.arange(expert_count, dtype=jnp.int32)
    onehot = (chosen[:, None] == expert_row[None, :]).astype(jnp.int32)
    before = jnp.cumsum(onehot, axis=0) - onehot
    slot_index = jnp.sum(before * onehot, axis=1)
    target_slot = chosen * CAP + slot_index
    targets = jnp.arange(expert_count * CAP, dtype=jnp.int32)
    matches = (target_slot[None, :] == targets[:, None]).astype(jnp.float32)
    matches = matches.reshape(expert_count * CAP, -1, 2)
    dispatch = jnp.sum(matches, axis=2)
    weights = numer_block.astype(jnp.float32) / denominator
    combine = jnp.sum(matches * weights[None, :, :], axis=2).T
    return (dispatch, combine)


def sign_table(order):
    position = lax.iota(jnp.int32, order)
    common = jnp.bitwise_and(position[:, None], position[None, :])
    parity_sum = jnp.zeros((order, order), jnp.int32)
    for bit_number in range(order.bit_length() - 1):
        parity_sum = parity_sum + jnp.bitwise_and(jnp.right_shift(common, bit_number), 1)
    return (1 - 2 * jnp.bitwise_and(parity_sum, 1)).astype(jnp.float32)


def shards(tokens, routes, gate_num, gate_weight, up_weight, down_weight):
    experts = lax.axis_size("expert")
    tensor_count = lax.axis_size("tensor")
    width_model = tokens.shape[1]
    dispatch, combine = slot_tables(routes, gate_num, experts)
    outgoing = jnp.dot(dispatch.astype(jnp.bfloat16), tokens, preferred_element_type=jnp.float32)
    outgoing = outgoing.astype(jnp.bfloat16).reshape(experts, CAP, width_model)
    arrived = lax.all_to_all(outgoing, "expert", split_axis=0, concat_axis=0, tiled=True)
    expert_rows = arrived.reshape(experts * CAP, width_model)
    gate_value = jnp.dot(expert_rows, gate_weight[0], preferred_element_type=jnp.float32)
    up_value = jnp.dot(expert_rows, up_weight[0], preferred_element_type=jnp.float32)
    hidden = (jax.nn.silu(gate_value) * up_value).astype(jnp.bfloat16)
    local_hidden = hidden.shape[1]
    norm_scale = 1.0 / math.sqrt(local_hidden * tensor_count)
    local_sign = sign_table(local_hidden).astype(jnp.bfloat16)
    transformed = jnp.dot(hidden, local_sign, preferred_element_type=jnp.float32)
    my_index = lax.axis_index("tensor")
    for bit_number in range(tensor_count.bit_length() - 1):
        partner = partner_2(transformed.astype(jnp.bfloat16), "tensor", bit_number).astype(
            transformed.dtype
        )
        lower_half = jnp.bitwise_and(jnp.right_shift(my_index, bit_number), 1) == 0
        transformed = jnp.where(lower_half, transformed + partner, partner - transformed)
    rotated = (transformed * norm_scale).astype(jnp.bfloat16)
    partial_value = jnp.dot(rotated, down_weight[0], preferred_element_type=jnp.float32)
    summed = lax.psum_scatter(
        partial_value.astype(jnp.bfloat16), "tensor", scatter_dimension=1, tiled=True
    ).astype(jnp.float32)
    returned_rows = lax.all_to_all(
        summed.reshape(experts, CAP, -1).astype(jnp.bfloat16),
        "expert",
        split_axis=0,
        concat_axis=0,
        tiled=True,
    ).astype(jnp.float32)
    token_rows = jnp.dot(
        combine,
        returned_rows.reshape(experts * CAP, -1),
        preferred_element_type=jnp.float32,
        precision=lax.Precision.HIGHEST,
    )
    return token_rows.astype(jnp.bfloat16)


def solution(mesh):
    placed = (
        P("expert", None),
        P("expert", None),
        P("expert", None),
        P("expert", None, "tensor"),
        P("expert", None, "tensor"),
        P("expert", "tensor", None),
    )
    return jax.shard_map(
        shards, mesh=mesh, in_specs=placed, out_specs=P("expert", "tensor"), check_vma=False
    )
```

profile of v0, /device:TPU:1, one launch (start us, length us, event | category | flops | bytes accessed | tf_op | source)
XLA Modules:
  0.0 418.6 jit_solution(10148921712858561632)
XLA Ops:
  6.5 0.9 copy.21
  7.6 0.1 eq.54
  7.8 0.6 reduce-window.6
  8.4 0.2 slice_reduce_fusion
  8.7 0.1 reduce_sum.30
  8.9 0.7 multiply_add_fusion
  9.6 0.7 convert_multiply_fusion
  10.3 0.8 convert_reduce_fusion
  11.1 3.2 convolution_convert_fusion.1
  14.3 78.1 %all_to_all.10 = bf16[8,64,6144]{2,1,0:T(8,128)(2,1)S(1)} all-to-all(bf16[8,64,6144]{2,1,0:T(8,128)(2,1)S(1)} %bitcast.35), channel_id=1, replica_groups=mesh['expert'=8,'tensor'=32] {'expert'}, dimensions={0} | all-to-all | bytes 12582912 | tf_op jit(solution)/shard_map/all_to_all | solution.py:50
  92.5 2.7 copy-done.1
  95.1 2.6 fusion.3
  97.7 6.8 %fusion.58 = (bf16[512,256]{1,0:T(8,128)(2,1)}, f32[512,256]{1,0:T(8,128)}) fusion(bf16[512,6144]{1,0:T(8,128)(2,1)} %bitcast.37, bf16[1,6144,256]{2,1,0:T(8,128)(2,1)} %param.10, f32[512,256]{1,0:T(8,128)} %fusion.3), kind=kOutput, calls=%fused_computation.73 | convolution fusion | flops 1680539648 | bytes 10747904 | tf_op jit(solution)/shard_map/dot_general | solution.py:58
  104.6 1.5 collective-permute-start
  106.0 5.5 %collective-permute-done = bf16[512,256]{1,0:T(8,128)(2,1)S(1)} collective-permute-done((bf16[512,256]{1,0:T(8,128)(2,1)}, bf16[512,256]{1,0:T(8,128)(2,1)S(1)}, u32[]{:S(2)}, u32[]{:S(2)}) %collective-permute-start) | collective-permute-done | bytes 262176 | tf_op jit(solution)/shard_map/ppermute | solution.py:15
  111.5 1.8 fusion.42
  113.4 3.2 collective-permute-start.1
  116.6 11.6 %collective-permute-done.1 = bf16[512,256]{1,0:T(8,128)(2,1)} collective-permute-done((bf16[512,256]{1,0:T(8,128)(2,1)}, bf16[512,256]{1,0:T(8,128)(2,1)}, u32[]{:S(2)}, u32[]{:S(2)}) %collective-permute-start.1) | collective-permute-done | bytes 262176 | tf_op jit(solution)/shard_map/ppermute | solution.py:15
  128.2 2.0 fusion.27
  130.2 6.4 %collective-permute-start.2 = (bf16[512,256]{1,0:T(8,128)(2,1)}, bf16[512,256]{1,0:T(8,128)(2,1)}, u32[]{:S(2)}, u32[]{:S(2)}) collective-permute-start(bf16[512,256]{1,0:T(8,128)(2,1)} %fusion.27), channel_id=1, source_target_pairs={{0,4},{1,5},{2,6},{3,7},{4,0},{5,1},{6,2},{7,3},{8,12},{9,13},{10,... | collective-permute-start | bytes 786440 | tf_op jit(solution)/shard_map/ppermute | solution.py:15
  136.6 8.9 %collective-permute-done.2 = bf16[512,256]{1,0:T(8,128)(2,1)} collective-permute-done((bf16[512,256]{1,0:T(8,128)(2,1)}, bf16[512,256]{1,0:T(8,128)(2,1)}, u32[]{:S(2)}, u32[]{:S(2)}) %collective-permute-start.2) | collective-permute-done | bytes 262176 | tf_op jit(solution)/shard_map/ppermute | solution.py:15
  145.5 2.3 fusion.56
  147.9 1.3 collective-permute-start.3
  149.2 4.1 collective-permute-done.3
  153.3 1.8 fusion.26
  155.1 2.9 collective-permute-start.4
  158.0 5.4 %collective-permute-done.4 = bf16[512,256]{1,0:T(8,128)(2,1)} collective-permute-done((bf16[512,256]{1,0:T(8,128)(2,1)}, bf16[512,256]{1,0:T(8,128)(2,1)}, u32[]{:S(2)}, u32[]{:S(2)}) %collective-permute-start.4) | collective-permute-done | bytes 262176 | tf_op jit(solution)/shard_map/ppermute | solution.py:15
  163.5 5.7 %convolution_convert_fusion = bf16[512,6144]{0,1:T(8,128)(2,1)} fusion(bf16[1,256,6144]{2,1,0:T(8,128)(2,1)S(1)} %copy-done, bf16[512,256]{1,0:T(8,128)(2,1)} %collective-permute-done.4, f32[512,256]{1,0:T(8,128)} %get-tuple-element.8, bf16[512,256]{1,0:T(8,128)(2,1)S(1)} %collective-permute-done.3, pred[]{:T(512)S(6)} %eq.66, pred[]{:T(512)S(6)} %eq.65), kind=kOutput, calls=%fused_computation | convolution fusion | flops 1615069184 | bytes 10485762 | tf_op jit(solution)/shard_map/dot_general | solution.py:67
  169.2 224.3 %reduce-scatter.2.cloned.1.call-done = bf16[512,192]{0,1:T(8,128)(2,1)} async-done(((bf16[512,6144]{0,1:T(8,128)(2,1)}), bf16[512,192]{0,1:T(8,128)(2,1)}) %reduce-scatter.2.cloned.1.call-update) | async-done | bytes 196624 | tf_op jit(solution)/shard_map/reduce_scatter | solution.py:68
  393.5 1.1 copy.24
  394.6 15.2 %all_to_all.11 = bf16[8,64,192]{2,1,0:T(8,128)(2,1)S(1)} all-to-all(bf16[8,64,192]{2,1,0:T(8,128)(2,1)S(1)} %bitcast.38), channel_id=1, replica_groups=mesh['expert'=8,'tensor'=32] {'expert'}, dimensions={0} | all-to-all | bytes 393216 | tf_op jit(solution)/shard_map/all_to_all | solution.py:71
  409.8 2.0 convolution_convert_fusion.2
  (13 shorter events, 0.4 us)
Async XLA Ops:
  6.5 156.9 %copy-start = (bf16[1,256,6144]{2,1,0:T(8,128)(2,1)S(1)}, bf16[1,256,6144]{2,1,0:T(8,128)(2,1)}, u32[]{:S(2)}) copy-start(bf16[1,256,6144]{2,1,0:T(8,128)(2,1)} %param.11) | copy-start | bytes 9437188
  6.5 387.0 %reduce-scatter.2.cloned.1.call-start = ((), (), s32[]{:S(2)}) async-start(), calls=%async_computation.3 | async-start | bytes 6488064 | tf_op jit(solution)/shard_map/reduce_scatter | solution.py:68
  14.3 80.8 %copy-start.2 = (bf16[1,6144,256]{2,1,0:T(8,128)(2,1)S(1)}, bf16[1,6144,256]{2,1,0:T(8,128)(2,1)}, u32[]{:S(2)}) copy-start(bf16[1,6144,256]{2,1,0:T(8,128)(2,1)} %param.9) | copy-start | bytes 9437188
  92.5 2.7 copy-start.1
  104.6 7.0 %collective-permute-start = (bf16[512,256]{1,0:T(8,128)(2,1)}, bf16[512,256]{1,0:T(8,128)(2,1)S(1)}, u32[]{:S(2)}, u32[]{:S(2)}) collective-permute-start(bf16[512,256]{1,0:T(8,128)(2,1)} %get-tuple-element.9), channel_id=1, source_target_pairs={{0,1},{1,0},{2,3},{3,2},{4,5},{5,4},{6,7},{7,6},{8,9},{9,8},{10,11... | collective-permute-start | bytes 786440 | tf_op jit(solution)/shard_map/ppermute | solution.py:15
  113.4 14.8 %collective-permute-start.1 = (bf16[512,256]{1,0:T(8,128)(2,1)}, bf16[512,256]{1,0:T(8,128)(2,1)}, u32[]{:S(2)}, u32[]{:S(2)}) collective-permute-start(bf16[512,256]{1,0:T(8,128)(2,1)} %fusion.42), channel_id=1, source_target_pairs={{0,2},{1,3},{2,0},{3,1},{4,6},{5,7},{6,4},{7,5},{8,10},{9,11},{10,... | collective-permute-start | bytes 786440 | tf_op jit(solution)/shard_map/ppermute | solution.py:15
  130.2 15.3 %collective-permute-start.2 = (bf16[512,256]{1,0:T(8,128)(2,1)}, bf16[512,256]{1,0:T(8,128)(2,1)}, u32[]{:S(2)}, u32[]{:S(2)}) collective-permute-start(bf16[512,256]{1,0:T(8,128)(2,1)} %fusion.27), channel_id=1, source_target_pairs={{0,4},{1,5},{2,6},{3,7},{4,0},{5,1},{6,2},{7,3},{8,12},{9,13},{10,... | collective-permute-start | bytes 786440 | tf_op jit(solution)/shard_map/ppermute | solution.py:15
  147.9 5.4 %collective-permute-start.3 = (bf16[512,256]{1,0:T(8,128)(2,1)}, bf16[512,256]{1,0:T(8,128)(2,1)S(1)}, u32[]{:S(2)}, u32[]{:S(2)}) collective-permute-start(bf16[512,256]{1,0:T(8,128)(2,1)} %get-tuple-element.7), channel_id=1, source_target_pairs={{0,8},{1,9},{2,10},{3,11},{4,12},{5,13},{6,14},{7,15},{8,0},{9,1},... | collective-permute-start | bytes 786440 | tf_op jit(solution)/shard_map/ppermute | solution.py:15
  155.1 8.4 %collective-permute-start.4 = (bf16[512,256]{1,0:T(8,128)(2,1)}, bf16[512,256]{1,0:T(8,128)(2,1)}, u32[]{:S(2)}, u32[]{:S(2)}) collective-permute-start(bf16[512,256]{1,0:T(8,128)(2,1)} %fusion.26), channel_id=1, source_target_pairs={{0,16},{1,17},{2,18},{3,19},{4,20},{5,21},{6,22},{7,23},{8,24},{9,... | collective-permute-start | bytes 786440 | tf_op jit(solution)/shard_map/ppermute | solution.py:15
Sparse Core Ops, SparseCore 0:
  169.4 224.0 reduce-scatter.1
where the time goes:
time: 419 us
  waiting for transfers between devices  260 us (62%)
  blocking collectives  93.4 us (22%)
  matrix products  20.3 us (5%)
  starting transfers between devices  15.3 us (4%)
  between operations  13.5 us (3%)
  other arithmetic  10.9 us (3%)
  local copies, waits for them, and re-layouts  5.36 us (1%)
    reduce_scatter x1, waiting for transfers between devices, shards(): lax.psum_scatter(partial_value.astype(jnp.bfloat16), 'tensor', scatter_di...  224 us
    all_to_all x1, blocking collectives, shards(): lax.all_to_all(outgoing, 'expert', split_axis=0, concat_axis=0, tiled=True)  78.1 us
    ppermute x5, waiting for transfers between devices, partner_2(): lax.ppermute(value, axis, [(i, i ^ 1 << apart) for i in range(lax.axis_si...  35.6 us
    ppermute x5, starting transfers between devices, partner_2(): lax.ppermute(value, axis, [(i, i ^ 1 << apart) for i in range(lax.axis_si...  15.3 us
    all_to_all x1, blocking collectives, shards(): lax.all_to_all(summed.reshape(experts, CAP, -1).astype(jnp.bfloat16), 'ex...  15.2 us
  transfers between devices with their start and end apart: 6, of which 6 were waited for; matrix products, arithmetic and copies ran while one was open for 0% of the time, Pallas kernels for 0%

commit v1 on v0

v1 whole, which is shorter than its diff:
```python
import math

import jax
import jax.numpy as jnp
from jax import lax
from jax.experimental import pallas as pl
from jax.experimental.pallas import tpu as pltpu
from jax.sharding import PartitionSpec as P

NX, NY, NZ, NT = 4, 4, 8, 32
CAP, TOK, D, HID = 64, 128, 6144, 256
YZ_COLS = NT * 128
MESH = pl.DeviceIdType.MESH
BF16, F32 = jnp.bfloat16, jnp.float32

GATHER_P, GATHER_Q = (128, 224), (352, 160)
REDUCE_P, REDUCE_Q = (0, 288), (288, 224)


class Node:
    def __init__(self, deps, cost, act=None, way=None, size=0, src=None, dst=None):
        self.deps, self.cost, self.act = list(deps), cost, act
        self.way, self.size, self.src, self.dst = way, size, src, dst


def steps_of(nodes):
    done, sent, steps, now, link, due = set(), set(), [], 0.0, {}, {}

    def send_ready():
        for i, node in enumerate(nodes):
            if node.way and i not in sent and all(d in done for d in node.deps):
                begin = max(now, link.get(node.way, 0.0))
                link[node.way] = begin + node.size * 2 / 1e5
                due[i] = link[node.way] + 1.6
                sent.add(i)
                steps.append(("send", i))

    send_ready()
    while len(done) < len(nodes):
        coming = sorted((due[i], i) for i in sent - done)
        tasks = [i for i, n in enumerate(nodes) if not n.way and i not in done and all(d in done for d in n.deps)]
        if coming and coming[0][0] <= now:
            pick = coming[0][1]
        elif tasks:
            pick = tasks[0]
        else:
            now, pick = coming[0]
        steps.append(("take" if nodes[pick].way else "task", pick))
        done.add(pick)
        now += nodes[pick].cost
        send_ready()
    return steps


def halves(rows):
    low, count = rows
    return (low, count // 2), (low + count // 2, count // 2)


def tree(p_rows, q_rows):
    found = []

    def add(way, slot, rows, deps):
        found.append((way, slot, rows, list(deps)))
        return len(found) - 1

    def ring(offset_y, rows, deps, arrived):
        for way, half in ((1, 0), (-1, 1)):
            before = deps
            for step in range(4):
                part = rows if step < 3 else halves(rows)[half]
                before = [add((0, way), (offset_y, -way * step), part, before)]
                arrived.setdefault(way * 4 if step == 3 else -way * (step + 1), []).extend(before)

    arrived = {}
    ring(0, p_rows, [], arrived)
    arrived = {0: [], 4: arrived.pop(4) + arrived.pop(-4), **arrived}
    for offset_z in (4, 3, -3, 2, -2, 1, -1, 0):
        up = add((1, 0), (0, offset_z), p_rows, arrived[offset_z])
        down = add((-1, 0), (0, offset_z), p_rows, arrived[offset_z])
        add((1, 0), (-1, offset_z), halves(p_rows)[0], [up])
        add((-1, 0), (1, offset_z), halves(p_rows)[1], [down])
    up = add((1, 0), (0, 0), q_rows, [])
    down = add((-1, 0), (0, 0), q_rows, [])
    far = [add((1, 0), (-1, 0), halves(q_rows)[0], [up]), add((-1, 0), (1, 0), halves(q_rows)[1], [down])]
    for offset_y, deps in ((0, []), (-1, [up]), (1, [down]), (2, far)):
        ring(offset_y, q_rows, deps, {})
    return found


def kernel(
    meta_ref, tok_ref, gate_ref, up_ref, down_ref, main_ref, extra_ref,
    metas, weights, downs, tiles, wide, acc, pick, blend, fold, mix, sent_rows, got_rows, back_rows, turned, mixed_in,
    part, part_in, cross, cross_in, over, over_in, last_in,
    a_send, a_recv, b_send, b_recv, c_send, c_recv, w_send, w_recv, w_own,
):
    own_e, own_t = lax.axis_index("expert"), lax.axis_index("tensor")
    x, c = lax.div(own_e, 2), lax.rem(own_e, 2)
    y, z = lax.div(own_t, NZ), lax.rem(own_t, NZ)

    def slot(dy, dz):
        return lax.rem(y + dy + NY, NY) * NZ + lax.rem(z + dz + NZ, NZ)

    def device(dx, dy, dz):
        return (lax.rem(x + dx + NX, NX) * 2 + c, slot(dy, dz))

    sibling = (x * 2 + 1 - c, own_t)

    barrier = pltpu.get_barrier_semaphore()
    for dx in (1, 2, 3):
        pl.semaphore_signal(barrier, inc=1, device_id=device(dx, 0, 0), device_id_type=MESH)
    pl.semaphore_signal(barrier, inc=1, device_id=sibling, device_id_type=MESH)

    def greet(k, carry):
        pl.semaphore_signal(barrier, inc=1, device_id=device(0, lax.div(k, NZ), lax.rem(k, NZ)), device_id_type=MESH)
        return carry

    lax.fori_loop(1, NT, greet, 0)

    def weight_part(number):
        group, which = number // 2, number % 2
        low = lax.rem(y + group, NY) * 1024 if group < 4 else 1024 * group
        return (gate_ref, up_ref)[which].at[pl.ds(low, 1024)], lambda expert: weights.at[expert, which, pl.ds(low, 1024)]

    def own_copy(number):
        if number < 12:
            src, dst = weight_part(number)
            return pltpu.make_async_copy(src, dst(0), w_own.at[number])
        return pltpu.make_async_copy(down_ref, downs.at[pl.ds(0, HID)], w_own.at[number])

    def sibling_copy(number):
        if number < 12:
            src, dst = weight_part(number)
            dst = dst(1)
        else:
            src, dst = down_ref, downs.at[pl.ds(HID, HID)]
        return pltpu.make_async_remote_copy(
            src_ref=src, dst_ref=dst, send_sem=w_send.at[number], recv_sem=w_recv.at[number],
            device_id=sibling, device_id_type=MESH,
        )

    for number in range(13):
        own_copy(number).start()

    def copy_of(node, number, send, recv):
        return pltpu.make_async_remote_copy(
            src_ref=node.src(), dst_ref=node.dst(), send_sem=send.at[number], recv_sem=recv.at[number],
            device_id=device(*node.way), device_id_type=MESH,
        )

    def run(nodes, send, recv):
        for kind, i in steps_of(nodes):
            if kind == "send":
                copy_of(nodes[i], i, send, recv).start()
            else:
                if kind == "take":
                    copy_of(nodes[i], i, send, recv).wait_recv()
                if nodes[i].act:
                    nodes[i].act()

    def finish(nodes, send, recv):
        for i, node in enumerate(nodes):
            if node.way:
                copy_of(node, i, send, recv).wait_send()

    nodes_a = []

    def message(nodes, way, size, src, dst, deps=(), act=None, cost=0.05):
        nodes.append(Node(deps, cost, act, way, size, src, dst))
        return len(nodes) - 1

    def task(nodes, act, deps, cost):
        nodes.append(Node(deps, cost, act))
        return len(nodes) - 1

    slices, meta_nodes = [], []
    for dx in (1, -1, 2):
        slices.append(message(
            nodes_a, (dx, 0, 0), 32768,
            lambda: tok_ref.at[:, pl.ds(pl.multiple_of(own_t * 128, 128), 128)],
            lambda dx=dx: tiles.at[own_t, pl.ds((-dx) % 4 * TOK, TOK)],
        ))
    for dx in (1, -1, 2):
        meta_nodes.append(message(
            nodes_a, (dx, 0, 0), 4096, lambda: meta_ref, lambda dx=dx: metas.at[(-dx) % 4],
        ))
    chunk_nodes = []
    for k in range(4):
        found = []
        for dx in (1, -1):
            found.append(message(
                nodes_a, (dx, 0, 0), 131072,
                lambda k=k: tok_ref.at[:, pl.ds(YZ_COLS + 512 * k, 512)],
                lambda k=k, dx=dx: wide.at[k, pl.ds((-dx) % 4 * TOK, TOK)],
            ))
        chunk_nodes.append(found)
    for k in range(4):
        dx = 1 if k < 2 else -1
        chunk_nodes[k].append(message(
            nodes_a, (dx, 0, 0), 131072,
            lambda k=k, dx=dx: wide.at[k, pl.ds((-dx) % 4 * TOK, TOK)],
            lambda k=k: wide.at[k, pl.ds(2 * TOK, TOK)],
            [chunk_nodes[k][0 if k < 2 else 1]],
        ))
    gather = tree(GATHER_P, GATHER_Q)
    base = len(nodes_a)
    group_nodes = [list(slices), [], [], []]
    for (dy, dz), (sy, sz), (low, count), deps in gather:
        def ref(sy=sy, sz=sz, low=low, count=count):
            return tiles.at[slot(sy, sz), pl.ds(low, count)]

        number = message(nodes_a, (0, dy, dz), count * 256, ref, ref, [base + d for d in deps] if deps else slices)
        group_nodes[(sy - dy) % 4].append(number)

    def expert_id(i):
        return 2 * x + (c if i == 0 else 1 - c)

    def fill():
        metas[0] = meta_ref[...]
        for number in range(13):
            sibling_copy(number).start()
        for t in range(NT):
            tiles[t, 0:TOK, :] = tok_ref[:, t * 128 : (t + 1) * 128]
        for k in range(4):
            wide[k, 0:TOK, :] = tok_ref[:, YZ_COLS + 512 * k : YZ_COLS + 512 * (k + 1)]

    def signs():
        def sign(row, column):
            common = row & column
            common = common ^ (common >> 4)
            common = common ^ (common >> 2)
            common = common ^ (common >> 1)
            return (1 - 2 * (common & 1)).astype(F32)

        def both(order):
            return lax.broadcasted_iota(jnp.int32, (order, order), 0), lax.broadcasted_iota(jnp.int32, (order, order), 1)

        row, column = both(HID)
        fold[...] = sign(row, column).astype(BF16)
        row, column = both(2 * HID)
        same = (row & 15) == (column & 15)
        mix[...] = jnp.where(same, sign(row >> 4, column >> 4), 0.0).astype(BF16)

    def tables():
        earlier = lax.broadcasted_iota(jnp.int32, (TOK, TOK), 0) < lax.broadcasted_iota(jnp.int32, (TOK, TOK), 1)
        earlier = earlier.astype(F32).astype(BF16)
        slots = lax.broadcasted_iota(jnp.int32, (CAP, TOK), 0).astype(F32)
        for dx in range(NX):
            first, second = metas[dx, 0:1, :], metas[dx, 1:2, :]
            gain_1, gain_2 = metas[dx, 2:3, :].astype(F32), metas[dx, 3:4, :].astype(F32)
            for i in range(2):
                is_1 = (first == expert_id(i)).astype(F32)
                is_2 = (second == expert_id(i)).astype(F32)
                named = is_1 + is_2
                place = jnp.dot(
                    jnp.broadcast_to(named, (16, TOK)).astype(BF16), earlier, preferred_element_type=F32
                )[0:1]
                hit = jnp.where(slots == place, 1.0, 0.0) * named
                pick[i, dx] = hit.astype(BF16)
                blend[i, dx] = (hit * ((is_1 * gain_1 + is_2 * gain_2) * (1.0 / 16.0))).astype(BF16)

    def weights_wait(group):
        for number in (2 * group, 2 * group + 1):
            own_copy(number).wait()
            sibling_copy(number).wait_recv()

    started = []

    def accumulate(rows, low, count):
        fresh = not started
        started.append(low)
        for i in range(2):
            for which in range(2):
                term = jnp.dot(rows, weights[i, which, pl.ds(low, count), :], preferred_element_type=F32)
                acc[i, which] = term if fresh else acc[i, which] + term

    def group_dot(group):
        weights_wait(group)
        base_y = lax.rem(y + group, NY)
        rows = jnp.concatenate([tiles[base_y * NZ + j] for j in range(NZ)], axis=1)
        accumulate(rows, base_y * 1024, 1024)

    def chunk_dot(k):
        if k % 2 == 0:
            weights_wait(4 + k // 2)
        accumulate(wide[k], YZ_COLS + 512 * k, 512)

    fill_task = task(nodes_a, fill, [], 0.6)
    sign_task = task(nodes_a, signs, [], 1.0)
    task(nodes_a, tables, meta_nodes + [fill_task], 0.6)
    last = sign_task
    for k in range(4):
        last = task(nodes_a, lambda k=k: chunk_dot(k), chunk_nodes[k] + [last], 0.6)
    for group in (0, 1, 3, 2):
        task(nodes_a, lambda group=group: group_dot(group), group_nodes[group] + [sign_task], 1.0)

    pl.semaphore_wait(barrier, NT - 1 + 4)
    run(nodes_a, a_send, a_recv)

    for i in range(2):
        gate, up = acc[i, 0], acc[i, 1]
        turned[...] = (gate / (1.0 + jnp.exp(-gate)) * up).astype(BF16)
        for dx in range(NX):
            chosen = jnp.dot(pick[i, dx], turned[dx * TOK : (dx + 1) * TOK, :], preferred_element_type=F32).astype(BF16)
            low = (i * NX + dx) * CAP
            sent_rows[low : low + CAP, :] = jnp.dot(chosen, fold[...], preferred_element_type=F32).astype(BF16)

    def piece(ref, t):
        return ref.at[pl.ds(pl.multiple_of(t * 16, 16), 16)]

    def exchange(src, dst, first):
        def copy(k):
            other = slot(lax.div(k, NZ), lax.rem(k, NZ))
            return pltpu.make_async_remote_copy(
                src_ref=piece(src, other), dst_ref=piece(dst, own_t),
                send_sem=b_send.at[first + k], recv_sem=b_recv.at[first + k],
                device_id=(own_e, other), device_id_type=MESH,
            )

        lax.fori_loop(1, NT, lambda k, u: (copy(k).start(), u)[1], 0)
        keep = pl.ds(pl.multiple_of(own_t * 16, 16), 16)
        dst[keep, :] = src[keep, :]
        lax.fori_loop(1, NT, lambda k, u: (copy(k).wait_recv(), u)[1], 0)
        return lambda: lax.fori_loop(1, NT, lambda k, u: (copy(k).wait_send(), u)[1], 0)

    sends_1 = exchange(sent_rows, got_rows, 0)
    values = jnp.dot(mix[...], got_rows[...], preferred_element_type=F32)
    back_rows[...] = (values * (1.0 / math.sqrt(NT * HID))).astype(BF16)
    sends_2 = exchange(back_rows, turned, NT)

    for i in range(2):
        for dx in range(NX):
            low = (i * NX + dx) * CAP
            spread = lax.dot_general(
                blend[i, dx], turned[low : low + CAP, :], (((0,), (0,)), ((), ())), preferred_element_type=F32
            )
            mixed_in[dx * TOK : (dx + 1) * TOK, i * HID : (i + 1) * HID] = spread.astype(BF16)
    own_copy(12).wait()
    sibling_copy(12).wait_recv()

    nodes_c = []

    def down_dot(group):
        base_y = lax.rem(y + group, NY)
        for half in range(2):
            columns = pl.ds(pl.multiple_of(base_y * 1536 + half * 768, 128), 768)
            values = jnp.dot(mixed_in[...], downs[:, columns], preferred_element_type=F32).astype(BF16)
            for pair in range(2):
                q = 2 * half + pair
                low = 384 * pair
                part[base_y * NZ + 2 * q] = values[:, low : low + 128]
                part[base_y * NZ + 2 * q + 1] = values[:, low + 256 : low + 384]
                for dx in range(NX):
                    cross[group, dx, q] = values[dx * TOK : (dx + 1) * TOK, low + 128 : low + 256]

    group_task = {}
    for group in (2, 1, 3, 0):
        group_task[group] = task(nodes_c, lambda group=group: down_dot(group), [], 1.0)

    base = len(nodes_c)
    reduction = tree(REDUCE_P, REDUCE_Q)
    total = 0
    roots = [group_task[0]]
    for number, ((dy, dz), (sy, sz), (low, count), deps) in enumerate(reduction):
        def src(sy=sy, sz=sz, dy=dy, dz=dz, low=low, count=count):
            return part.at[slot(sy - dy, sz - dz), pl.ds(low, count)]

        def dst(total=total, count=count):
            return part_in.at[pl.ds(total, count)]

        def act(sy=sy, sz=sz, low=low, count=count, total=total):
            here = slot(sy, sz)
            part[here, low : low + count, :] = part[here, low : low + count, :] + part_in[total : total + count, :]

        children = [base + n for n, other in enumerate(reduction) if number in other[3]]
        if not deps:
            roots.append(base + number)
        message(
            nodes_c, (0, -dy, -dz), count * 256, src, dst, children + [group_task[(sy - dy) % 4]], act, 0.1
        )
        total += count

    packed = {}
    for group in (2, 1, 3, 0):
        def add_cross(dx, low, count, index, group=group):
            for q in range(low, low + count):
                cross[group, dx, q] = cross[group, dx, q] + cross_in[group, index, q]

        def hop(way, dx, low, count, index, into, deps, group=group, add_cross=add_cross):
            return message(
                nodes_c, (way, 0, 0), count * 32768,
                lambda: cross.at[group, dx, pl.ds(low, count)],
                lambda: cross_in.at[group, index, pl.ds(low, count)],
                deps, lambda: add_cross(into, low, count, index), 0.2,
            )

        ready = group_task[group]
        far_1 = hop(-1, 2, 0, 2, 0, 3, [ready])
        far_2 = hop(1, 2, 2, 2, 0, 1, [ready])
        near_1 = hop(-1, 3, 0, 4, 1, 0, [ready, far_1])
        near_2 = hop(1, 1, 0, 4, 2, 0, [ready, far_2])

        def pack(group=group):
            lane = lax.broadcasted_iota(jnp.int32, (CAP, 128), 1)
            for q in range(4):
                top, low = cross[group, 0, q, 0:CAP, :].astype(F32), cross[group, 0, q, CAP:TOK, :].astype(F32)
                over[group, 2 * q] = jnp.where(lane < 64, top, pltpu.roll(low, 64, 1)).astype(BF16)
                over[group, 2 * q + 1] = jnp.where(lane < 64, pltpu.roll(top, 64, 1), low).astype(BF16)

        packed[group] = task(nodes_c, pack, [near_1, near_2, ready], 0.3)

    def add_over(group, low, count, index):
        for n in range(low, low + count):
            over[group, n] = over[group, n] + over_in[index, n]

    def over_hop(way, group, low, count, index, into, deps):
        return message(
            nodes_c, (0, way, 0), count * 16384,
            lambda: over.at[group, pl.ds(low, count)], lambda: over_in.at[index, pl.ds(low, count)],
            deps, lambda: add_over(into, low, count, index), 0.1,
        )

    far_1 = over_hop(-1, 2, 0, 4, 0, 3, [packed[2]])
    far_2 = over_hop(1, 2, 4, 4, 0, 1, [packed[2]])
    near_1 = over_hop(-1, 3, 0, 8, 1, 0, [packed[3], far_1])
    near_2 = over_hop(1, 1, 0, 8, 2, 0, [packed[1], far_2])
    ends = []
    for way, low, index in ((1, 0, 3), (-1, 32, 4)):
        before = [near_1, near_2, packed[0]]
        for step in (3, 2, 1, 0):
            rows = pl.ds(low, 32) if step == 3 else pl.ds(0, CAP)

            def src(way=way, step=step, rows=rows):
                return over.at[0, lax.rem(z - way * (step + 1) + NZ, NZ), rows]

            def dst(step=step, rows=rows, index=index):
                return over_in.at[index, step, rows]

            def act(way=way, step=step, rows=rows, index=index):
                here = lax.rem(z - way * step + NZ, NZ)
                over[0, here, rows, :] = over[0, here, rows, :] + over_in[index, step, rows, :]

            size = (32 if step == 3 else CAP) * 256
            before = [near_1, near_2, packed[0], message(nodes_c, (0, 0, -way), size, src, dst, before, act, 0.05)]
        ends.append(before[-1])

    lasts = []
    for dx in (2, 1, -1):
        lasts.append(message(
            nodes_c, (dx, 0, 0), 32768, lambda dx=dx: part.at[own_t, pl.ds(dx % 4 * TOK, TOK)],
            lambda dx=dx: last_in.at[(-dx) % 4], roots,
        ))

    def store():
        summed = part[own_t, 0:TOK, :].astype(F32)
        for dx in (1, 2, 3):
            summed = summed + last_in[dx].astype(F32)
        main_ref[...] = summed.astype(BF16)
        extra_ref[...] = over[0, z]

    task(nodes_c, store, lasts + ends, 0.2)
    run(nodes_c, c_send, c_recv)

    finish(nodes_a, a_send, a_recv)
    for number in range(13):
        sibling_copy(number).wait_send()
    sends_1()
    sends_2()
    finish(nodes_c, c_send, c_recv)


def shards(tokens, routes, gate_num, gate_weight, up_weight, down_weight):
    meta = jnp.concatenate([routes.T, gate_num.T, jnp.zeros((4, TOK), jnp.int32)], axis=0)
    vmem, anywhere = pl.BlockSpec(memory_space=pltpu.VMEM), pl.BlockSpec(memory_space=pl.ANY)
    dma = pltpu.SemaphoreType.DMA
    main, extra = pl.pallas_call(
        kernel,
        out_shape=(jax.ShapeDtypeStruct((TOK, 128), BF16), jax.ShapeDtypeStruct((CAP, 128), BF16)),
        in_specs=[vmem, vmem, anywhere, anywhere, anywhere],
        out_specs=(vmem, vmem),
        scratch_shapes=[
            pltpu.VMEM((NX, 8, TOK), jnp.int32),
            pltpu.VMEM((2, 2, D, HID), BF16),
            pltpu.VMEM((2 * HID, D), BF16),
            pltpu.VMEM((NT, NX * TOK, 128), BF16),
            pltpu.VMEM((4, NX * TOK, 512), BF16),
            pltpu.VMEM((2, 2, NX * TOK, HID), F32),
            pltpu.VMEM((2, NX, CAP, TOK), BF16),
            pltpu.VMEM((2, NX, CAP, TOK), BF16),
            pltpu.VMEM((HID, HID), BF16),
            pltpu.VMEM((2 * HID, 2 * HID), BF16),
            pltpu.VMEM((2 * NX * CAP, HID), BF16),
            pltpu.VMEM((2 * NX * CAP, HID), BF16),
            pltpu.VMEM((2 * NX * CAP, HID), BF16),
            pltpu.VMEM((2 * NX * CAP, HID), BF16),
            pltpu.VMEM((NX * TOK, 2 * HID), BF16),
            pltpu.VMEM((NT, NX * TOK, 128), BF16),
            pltpu.VMEM((15872, 128), BF16),
            pltpu.VMEM((4, NX, 4, TOK, 128), BF16),
            pltpu.VMEM((4, 3, 4, TOK, 128), BF16),
            pltpu.VMEM((4, NZ, CAP, 128), BF16),
            pltpu.VMEM((5, NZ, CAP, 128), BF16),
            pltpu.VMEM((NX, TOK, 128), BF16),
            dma((100,)), dma((100,)), dma((64,)), dma((64,)), dma((128,)), dma((128,)),
            dma((13,)), dma((13,)), dma((13,)),
        ],
        compiler_params=pltpu.CompilerParams(
            collective_id=0, has_side_effects=True, vmem_limit_bytes=60 * 2**20
        ),
        cost_estimate=pl.CostEstimate(flops=10**10, bytes_accessed=2 * 10**7, transcendentals=2**18),
        name="moe_layer",
    )(meta, tokens, gate_weight[0], up_weight[0], down_weight[0])
    extra = jnp.concatenate([extra[:, :64], extra[:, 64:]], axis=0)
    odd = lax.rem(lax.axis_index("tensor"), 2) == 1
    return jnp.where(odd, jnp.concatenate([extra, main], axis=1), jnp.concatenate([main, extra], axis=1))


def solution(mesh):
    placed = (
        P("expert", None),
        P("expert", None),
        P("expert", None),
        P("expert", None, "tensor"),
        P("expert", None, "tensor"),
        P("expert", "tensor", None),
    )
    return jax.shard_map(
        shards, mesh=mesh, in_specs=placed, out_specs=P("expert", "tensor"), check_vma=False
    )
```

time: 419 us -> 114 us (0.27)
  the two profiles are of different devices: /device:TPU:1 before, /device:TPU:6 now
where the time goes in v1:
time: 114 us; the launch traced here: 113 us
  Pallas kernels  109 us (96%)
  other arithmetic  2.28 us (2%)
  local copies, waits for them, and re-layouts  1.67 us (1%)
    pallas_call x1, Pallas kernels, shards(): pl.pallas_call(kernel, out_shape=(jax.ShapeDtypeStruct((TOK, 128), BF16),...  109 us

profile of v1, /device:TPU:6, one launch (start us, length us, event | category | flops | bytes accessed | tf_op | source)
XLA Modules:
  0.0 113.3 jit_solution(4145157041452954277)
XLA Ops:
  0.0 0.1 pad.8.clone
  0.1 1.4 %add_add_fusion.meta_ref = s32[8,128]{1,0:T(8,128)} fusion(s32[2,128]{1,0:T(2,128)} %bitcast.5, s32[2,128]{1,0:T(2,128)} %bitcast.6, s32[8]{0:T(128)S(1)} %pad.8.clone), kind=kLoop, calls=%fused_computation.1 | loop fusion | flops 2048 | bytes 6176 | tf_op jit(solution)/shard_map/concatenate | solution.py:473
  1.4 109.3 %moe_layer.1 = (bf16[128,128]{1,0:T(8,128)(2,1)}, bf16[64,128]{1,0:T(8,128)(2,1)}) custom-call(s32[8,128]{1,0:T(8,128)} %add_add_fusion.meta_ref, bf16[128,6144]{1,0:T(8,128)(2,1)} %tok_ref.1, bf16[6144,256]{1,0:T(8,128)(2,1)} %bitcast.7, bf16[6144,256]{1,0:T(8,128)(2,1)} %bitcast.8, bf16[256,6144]{1,0:T(8,128)(2,1)} %bitcast.9), custom_call_target="tpu_custom_call" | custom-call | flops 10000000000 | bytes 20000000 | tf_op jit(solution)/shard_map/moe_layer/pallas_call | solution.py:476
  110.8 0.9 fusion
  111.7 0.9 maximum_select_fusion
  112.6 0.7 copy.7
  (1 shorter events, 0.0 us)

commit v2 on v0

v2 whole, which is shorter than its diff:
```python
import math

import jax
import jax.numpy as jnp
from jax import lax
from jax.experimental import pallas as pl
from jax.experimental.pallas import tpu as pltpu
from jax.sharding import PartitionSpec as P

NX, NY, NZ, NT = 4, 4, 8, 32
CAP, TOK, D, HID = 64, 128, 6144, 256
YZ_COLS = NT * 128
MESH = pl.DeviceIdType.MESH
BF16, F32 = jnp.bfloat16, jnp.float32

PEERS = tuple((dx, dc) for dx in (0, 2, 1, 3) for dc in (0, 1))
GATHER = ((128, 224), (352, 160))
REDUCE = ((0, 288), (288, 224))
LATENCY, B_PAUSE = 2.2, 6.0


class Node:
    def __init__(self, deps, cost, act=None, way=None, size=0, src=None, dst=None, pause=0.0, bundle=None, sender=None):
        self.deps, self.cost, self.act, self.pause = list(deps), cost, act, pause
        self.way, self.size, self.src, self.dst, self.bundle, self.sender = way, size, src, dst, bundle, sender


def steps_of(nodes):
    done, sent, steps, now, link, due = set(), set(), [], 0.0, {}, {}

    def occupy(way, size):
        end = now
        for axis, hops in enumerate(way[:3]):
            both = abs(hops) * 2 == (NX, NY, NZ)[axis]
            for sign in (1, -1) if both else (1,) if hops > 0 else (-1,):
                if hops:
                    key = (axis, sign)
                    link[key] = max(now, link.get(key, 0.0)) + size * 2 / 1e5 * abs(hops) / (2 if both else 1)
                    end = max(end, link[key])
        return end + 0.6 * max(0, sum(abs(hops) for hops in way[:3]) - 1)

    def send_ready():
        for i, node in enumerate(nodes):
            if i not in due and all(d in done for d in node.deps):
                if node.way:
                    due[i] = occupy(node.way, node.size) + LATENCY
                    sent.add(i)
                    steps.append(("send", i))
                else:
                    due[i] = now + node.pause

    send_ready()
    while len(done) < len(nodes):
        ready = [(due[i], i) for i in due if i not in done]
        arrived = [r for r in ready if r[1] in sent and r[0] <= now]
        tasks = [r[1] for r in ready if r[1] not in sent and r[0] <= now]
        if arrived:
            pick = min(arrived)[1]
        elif tasks:
            pick = min(tasks)
        else:
            now, pick = min(ready)
        steps.append(("take" if nodes[pick].way else "task", pick))
        done.add(pick)
        now += nodes[pick].cost
        send_ready()
    return steps


def halves(rows):
    low, count = rows
    return (low, count // 2), (low + count // 2, count // 2)


def tree(p_rows, q_rows):
    found = []

    def add(way, slot, rows, deps):
        found.append((way, slot, rows, list(deps)))
        return len(found) - 1

    def ring(offset_y, rows, deps, arrived):
        for way, half in ((1, 0), (-1, 1)):
            before = deps
            for step in range(4):
                part = rows if step < 3 else halves(rows)[half]
                before = [add((0, way), (offset_y, -way * step), part, before)]
                arrived.setdefault(way * 4 if step == 3 else -way * (step + 1), []).extend(before)

    arrived = {}
    ring(0, p_rows, [], arrived)
    arrived = {0: [], 4: arrived.pop(4) + arrived.pop(-4), **arrived}
    for offset_z in (4, 3, -3, 2, -2, 1, -1, 0):
        up = add((1, 0), (0, offset_z), p_rows, arrived[offset_z])
        down = add((-1, 0), (0, offset_z), p_rows, arrived[offset_z])
        add((1, 0), (-1, offset_z), halves(p_rows)[0], [up])
        add((-1, 0), (1, offset_z), halves(p_rows)[1], [down])
    up = add((1, 0), (0, 0), q_rows, [])
    down = add((-1, 0), (0, 0), q_rows, [])
    far = [add((1, 0), (-1, 0), halves(q_rows)[0], [up]), add((-1, 0), (1, 0), halves(q_rows)[1], [down])]
    for offset_y, deps in ((0, []), (-1, [up]), (1, [down]), (2, far)):
        ring(offset_y, q_rows, deps, {})
    return found


def kernel(
    routes_ref, gains_ref, tok_ref, gate_ref, up_ref, down_ref, out_ref,
    weights, downs, tiles, wide, sliced, chunked, near, acc, pick, blend, fold, mix,
    sent_rows, got_rows, back_rows, turned, part, part_in, cross, cross_in, over, over_in, over_last, last_in,
    sends, recvs, b_send, b_recv, w_own,
):
    own_e, own_t = lax.axis_index("expert"), lax.axis_index("tensor")
    x, c = lax.div(own_e, 2), lax.rem(own_e, 2)
    y, z = lax.div(own_t, NZ), lax.rem(own_t, NZ)

    def slot(dy, dz):
        return lax.rem(y + dy + NY, NY) * NZ + lax.rem(z + dz + NZ, NZ)

    def device(dx, dy, dz, dc=0):
        return (lax.rem(x + dx + NX, NX) * 2 + (1 - c if dc else c), slot(dy, dz))

    barrier = pltpu.get_barrier_semaphore()
    for dx, dc in PEERS[1:]:
        pl.semaphore_signal(barrier, inc=1, device_id=device(dx, 0, 0, dc), device_id_type=MESH)

    def greet(k, carry):
        pl.semaphore_signal(barrier, inc=1, device_id=device(0, lax.div(k, NZ), lax.rem(k, NZ)), device_id_type=MESH)
        return carry

    lax.fori_loop(1, NT, greet, 0)

    areas = (pl.ds(YZ_COLS, D - YZ_COLS), pl.ds(0, YZ_COLS))

    def own_copy(number):
        if number < 4:
            area, which = areas[number // 2], number % 2
            return pltpu.make_async_copy(
                (gate_ref, up_ref)[which].at[area], weights.at[which, area], w_own.at[number]
            )
        return pltpu.make_async_copy(down_ref, downs, w_own.at[number])

    for number in range(5):
        own_copy(number).start()

    nodes = []

    def message(way, size, src, dst, deps=(), act=None, cost=0.04, bundle=None, sender=0):
        nodes.append(Node(deps, cost, act, way, size, src, dst, bundle=bundle, sender=sender))
        return len(nodes) - 1

    def task(act, deps, cost, pause=0.0):
        nodes.append(Node(deps, cost, act, pause=pause))
        return len(nodes) - 1

    def sign(row, column):
        common = row & column
        common = common ^ (common >> 4)
        common = common ^ (common >> 2)
        common = common ^ (common >> 1)
        return (1 - 2 * (common & 1)).astype(F32)

    def iotas(rows, columns):
        shape = (rows, columns)
        return lax.broadcasted_iota(jnp.int32, shape, 0), lax.broadcasted_iota(jnp.int32, shape, 1)

    def lands(dx, dc):
        return PEERS.index((-dx % 4, dc))

    def peer_way(number):
        dx, dc = PEERS[number]
        return (-1 if dx == 3 else dx, 0, 0, dc)

    def tables():
        row, column = iotas(TOK, TOK)
        earlier = (row < column).astype(F32).astype(BF16)
        slots = iotas(CAP, TOK)[0].astype(F32)
        first, second = routes_ref[0:1, :], routes_ref[1:2, :]
        gain_1, gain_2 = gains_ref[0:1, :].astype(F32), gains_ref[1:2, :].astype(F32)
        for number, (dx, dc) in enumerate(PEERS):
            expert = device(dx, 0, 0, dc)[0]
            is_1, is_2 = (first == expert).astype(F32), (second == expert).astype(F32)
            named = is_1 + is_2
            place = jnp.dot(
                jnp.broadcast_to(named, (16, TOK)).astype(BF16), earlier, preferred_element_type=F32
            )[0:1]
            hit = jnp.where(slots == place, 1.0, 0.0) * named
            area = slice(number * CAP, (number + 1) * CAP)
            pick[area, :] = hit.astype(BF16)
            blend[area, :] = (hit * ((is_1 * gain_1 + is_2 * gain_2) * (1.0 / 16.0))).astype(BF16)

    def slice_rows():
        columns = pl.ds(pl.multiple_of(own_t * 128, 128), 128)
        sliced[...] = jnp.dot(pick[...], tok_ref[:, columns], preferred_element_type=F32).astype(BF16)

    def chunk_rows(low, high):
        for k in range(4):
            columns = tok_ref[:, YZ_COLS + 512 * k : YZ_COLS + 512 * (k + 1)]
            area = slice(low * CAP, high * CAP)
            rows = jnp.dot(pick[area, :], columns, preferred_element_type=F32).astype(BF16)
            for number in range(low, high):
                piece = rows[(number - low) * CAP : (number - low + 1) * CAP]
                if number == 0:
                    wide[k, 0:CAP, :] = piece
                else:
                    chunked[k, number] = piece

    def near_rows():
        for t in range(NT):
            columns = tok_ref[:, t * 128 : (t + 1) * 128]
            rows = jnp.dot(pick[0 : 2 * CAP, :], columns, preferred_element_type=F32).astype(BF16)
            tiles[t, 0:CAP, :] = rows[0:CAP]
            near[t] = rows[CAP : 2 * CAP]

    tables()
    slice_rows()
    chunk_rows(0, 8)
    near_task = task(near_rows, [], 0.5)

    slices, chunk_nodes = [], []
    for number in (2, 3, 4, 5, 6, 7):
        slices.append(message(
            peer_way(number), 16384,
            lambda number=number: sliced.at[pl.ds(number * CAP, CAP)],
            lambda number=number: tiles.at[own_t, pl.ds(lands(*PEERS[number]) * CAP, CAP)],
            bundle="slices",
        ))
    for k in range(4):
        chunk_nodes.append([
            message(
                peer_way(number), 65536,
                lambda k=k, number=number: chunked.at[k, number],
                lambda k=k, number=number: wide.at[k, pl.ds(lands(*PEERS[number]) * CAP, CAP)],
                bundle=("chunk", k),
            )
            for number in (2, 3, 4, 5, 6, 7, 1)
        ])
    near_node = message(
        (0, 0, 0, 1), 524288, lambda: near, lambda: tiles.at[pl.ds(0, NT), pl.ds(CAP, CAP)], [near_task]
    )
    group_nodes = [list(slices), [], [], []]
    base = len(nodes)
    for (dy, dz), (sy, sz), (low, count), deps in tree(*GATHER):
        def ref(sy=sy, sz=sz, low=low, count=count):
            return tiles.at[slot(sy, sz), pl.ds(low, count)]

        number = message((0, dy, dz), count * 256, ref, ref, [base + d for d in deps] if deps else slices, sender=1)
        group_nodes[(sy - dy) % 4].append(number)

    def fold_signs():
        fold[...] = sign(*iotas(HID, HID)).astype(BF16)

    def mix_signs(low):
        row, column = iotas(2 * CAP, 2 * HID)
        row = row + low
        mix[low : low + 2 * CAP, :] = jnp.where(
            (row & 15) == (column & 15), sign(row >> 4, column >> 4), 0.0
        ).astype(BF16)

    fold_task = task(fold_signs, [near_task], 0.1)
    mix_tasks = [task(lambda n=n: mix_signs(n * 2 * CAP), [fold_task], 0.05) for n in range(4)]

    def weights_wait(low):
        own_copy(low).wait()
        own_copy(low + 1).wait()

    wide_weights = task(lambda: weights_wait(0), [near_task], 0.02)
    tile_weights = task(lambda: weights_wait(2), [wide_weights], 0.02)

    started = []

    def accumulate(rows, low, count):
        fresh = not started
        started.append(low)
        for which in range(2):
            term = jnp.dot(rows, weights[which, pl.ds(low, count), :], preferred_element_type=F32)
            acc[which] = term if fresh else acc[which] + term

    def group_dot(group):
        base_y = lax.rem(y + group, NY)
        rows = jnp.concatenate([tiles[base_y * NZ + j] for j in range(NZ)], axis=1)
        accumulate(rows, base_y * 1024, 1024)

    def chunk_dot(k):
        accumulate(wide[k], YZ_COLS + 512 * k, 512)

    def hide():
        gate, up = acc[0], acc[1]
        hidden = (gate / (1.0 + jnp.exp(-gate)) * up).astype(BF16)
        sent_rows[...] = jnp.dot(hidden, fold[...], preferred_element_type=F32).astype(BF16)

    def piece(t):
        return pl.ds(pl.multiple_of(t * 16, 16), 16)

    def start_all(src, dst, turn):
        def start(k, carry):
            other = slot(lax.div(k, NZ), lax.rem(k, NZ))
            pltpu.make_async_remote_copy(
                src_ref=src.at[piece(other)], dst_ref=dst.at[piece(own_t)],
                send_sem=b_send.at[turn], recv_sem=b_recv.at[turn],
                device_id=(own_e, other), device_id_type=MESH,
            ).start()
            return carry

        lax.fori_loop(1, NT, start, 0)
        dst[piece(own_t), :] = src[piece(own_t), :]

    def all_of(ref, turn):
        area = ref.at[pl.ds(0, (NT - 1) * 16)]
        return pltpu.make_async_remote_copy(
            src_ref=area, dst_ref=area, send_sem=b_send.at[turn], recv_sem=b_recv.at[turn],
            device_id=(own_e, slot(0, 1)), device_id_type=MESH,
        )

    def rotate():
        all_of(got_rows, 0).wait_recv()
        values = jnp.dot(mix[...], got_rows[...], preferred_element_type=F32)
        back_rows[...] = (values * (1.0 / math.sqrt(NT * HID))).astype(BF16)
        start_all(back_rows, turned, 1)

    dots = [task(lambda k=k: chunk_dot(k), chunk_nodes[k] + [wide_weights], 0.5) for k in range(4)]
    for group in (0, 1, 3, 2):
        dots.append(task(
            lambda group=group: group_dot(group),
            group_nodes[group] + [tile_weights, near_node, near_task], 0.9,
        ))
    hidden_task = task(hide, dots + [fold_task], 1.0)
    gone = task(lambda: start_all(sent_rows, got_rows, 0), [hidden_task], 1.0)
    back = task(rotate, [gone] + mix_tasks, 1.5, B_PAUSE)
    come = task(lambda: all_of(turned, 1).wait_recv(), [back], 0.1, B_PAUSE)

    down_task = task(lambda: own_copy(4).wait(), [tile_weights], 0.02)

    def down_dot(group):
        base_y = lax.rem(y + group, NY)
        for side in range(2):
            columns = pl.ds(pl.multiple_of(base_y * 1536 + side * 768, 128), 768)
            values = jnp.dot(turned[...], downs[:, columns], preferred_element_type=F32).astype(BF16)
            for pair in range(2):
                q = 2 * side + pair
                low = 384 * pair
                part[base_y * NZ + 2 * q] = values[:, low : low + 128]
                part[base_y * NZ + 2 * q + 1] = values[:, low + 256 : low + 384]
                for number in range(8):
                    into = cross_in if number == 0 else cross
                    into[group, number, q] = values[number * CAP : (number + 1) * CAP, low + 128 : low + 256]

    group_task, cross_nodes = {}, {}
    for group in (2, 1, 3, 0):
        group_task[group] = task(lambda group=group: down_dot(group), [come, down_task], 0.8)
        cross_nodes[group] = [
            message(
                peer_way(n), 65536, lambda group=group, n=n: cross.at[group, n],
                lambda group=group, n=n: cross_in.at[group, lands(*PEERS[n])],
                [group_task[group]], bundle=("cross", group), sender=2,
            )
            for n in (2, 3, 4, 5, 6, 7, 1)
        ]

    def blended(rows):
        return lax.dot_general(blend[...], rows, (((0,), (0,)), ((), ())), preferred_element_type=F32)

    packed = {}
    for group in (2, 1, 3, 0):
        def pack(group=group):
            lane = iotas(CAP, 128)[1]
            for q in range(4):
                sums = blended(cross_in[group, 0:8, q].reshape(8 * CAP, 128))
                top, low = sums[0:CAP], sums[CAP:TOK]
                over[group, 2 * q] = jnp.where(lane < 64, top, pltpu.roll(low, 64, 1)).astype(BF16)
                over[group, 2 * q + 1] = jnp.where(lane < 64, pltpu.roll(top, 64, 1), low).astype(BF16)

        packed[group] = task(pack, cross_nodes[group] + [group_task[group]], 0.4)

    over_nodes = [
        message(
            (0, -1 if group == 3 else group, 0), 131072, lambda group=group: over.at[group],
            lambda group=group: over_in.at[group - 1], [packed[group]], sender=2,
        )
        for group in (2, 1, 3)
    ]

    def add_over():
        for n in range(NZ):
            sums = over[0, n].astype(F32)
            for index in range(3):
                sums = sums + over_in[index, n].astype(F32)
            over[0, n] = sums.astype(BF16)

    over_task = task(add_over, over_nodes + [packed[0]], 0.3)
    ends = [
        message(
            (0, 0, dz), 16384, lambda dz=dz: over.at[0, lax.rem(z + dz + NZ, NZ)],
            lambda dz=dz: over_last.at[dz % NZ - 1], [over_task], bundle="over", sender=2,
        )
        for dz in (4, 3, -3, 2, -2, 1, -1)
    ]

    total, base = 0, len(nodes)
    reduction = tree(*REDUCE)
    roots = [group_task[0]]
    for number, ((dy, dz), (sy, sz), (low, count), deps) in enumerate(reduction):
        def src(sy=sy, sz=sz, dy=dy, dz=dz, low=low, count=count):
            return part.at[slot(sy - dy, sz - dz), pl.ds(low, count)]

        def dst(total=total, count=count):
            return part_in.at[pl.ds(total, count)]

        def act(sy=sy, sz=sz, low=low, count=count, total=total):
            here = slot(sy, sz)
            part[here, low : low + count, :] = part[here, low : low + count, :] + part_in[total : total + count, :]

        children = [base + n for n, other in enumerate(reduction) if number in other[3]]
        if not deps:
            roots.append(base + number)
        needs = [group_task[(sy - dy) % 4], group_task[sy % 4]]
        message((0, -dy, -dz), count * 256, src, dst, children + needs, act, count / 4000, sender=3)
        total += count
    lasts = [
        message(
            peer_way(n), 16384, lambda n=n: part.at[own_t, pl.ds(n * CAP, CAP)],
            lambda n=n: last_in.at[pl.ds(lands(*PEERS[n]) * CAP, CAP)], roots, bundle="last", sender=2,
        )
        for n in (2, 3, 4, 5, 6, 7, 1)
    ]

    def store():
        last_in[0:CAP, :] = part[own_t, 0:CAP, :]
        summed = blended(last_in[...])
        rolled = pltpu.roll(summed, 64, 1)
        extra = over[0, z].astype(F32)
        for index in range(NZ - 1):
            extra = extra + over_last[index].astype(F32)
        extra = jnp.concatenate([extra, pltpu.roll(extra, 64, 1)], axis=0)
        odd = lax.rem(own_t, 2) == 1
        lane = iotas(TOK, 128)[1]
        left = jnp.where(odd, jnp.where(lane < 64, extra, rolled), summed)
        right = jnp.where(odd, rolled, extra)
        out_ref[:, 0:128] = left.astype(BF16)
        out_ref[:, 128:192] = right[:, 0:64].astype(BF16)

    task(store, lasts + ends, 0.2)

    marks = []
    for number, node in enumerate(nodes):
        if node.way:
            key = node.bundle or number
            if key not in marks:
                marks.append(key)

    def copy_of(number, src=None, dst=None):
        node = nodes[number]
        return pltpu.make_async_remote_copy(
            src_ref=src or node.src(), dst_ref=dst or node.dst(),
            send_sem=sends.at[node.sender], recv_sem=recvs.at[marks.index(node.bundle or number)],
            device_id=device(*node.way), device_id_type=MESH,
        )

    def rows_of(chosen):
        return part_in.at[pl.ds(0, sum(node.size for node in chosen) // 256)]

    pl.semaphore_wait(barrier, NT - 1 + 7)
    taken = {}
    for kind, number in steps_of(nodes):
        node = nodes[number]
        if kind == "send":
            copy_of(number).start()
            continue
        if kind == "take" and node.bundle:
            members = [other for other in nodes if other.bundle == node.bundle]
            taken[node.bundle] = taken.get(node.bundle, 0) + 1
            if taken[node.bundle] == len(members):
                area = rows_of(members)
                copy_of(number, area, area).wait_recv()
        elif kind == "take":
            copy_of(number).wait_recv()
        if node.act:
            node.act()

    for sender in range(4):
        chosen = [number for number, node in enumerate(nodes) if node.way and node.sender == sender]
        area = rows_of([nodes[number] for number in chosen])
        copy_of(chosen[0], area, area).wait_send()
    for turn in range(2):
        all_of(back_rows, turn).wait_send()


def shards(tokens, routes, gate_num, gate_weight, up_weight, down_weight):
    vmem, anywhere = pl.BlockSpec(memory_space=pltpu.VMEM), pl.BlockSpec(memory_space=pl.ANY)
    dma = pltpu.SemaphoreType.DMA
    return pl.pallas_call(
        kernel,
        out_shape=jax.ShapeDtypeStruct((TOK, 192), BF16),
        in_specs=[vmem, vmem, vmem, anywhere, anywhere, anywhere],
        out_specs=vmem,
        scratch_shapes=[
            pltpu.VMEM((2, D, HID), BF16),
            pltpu.VMEM((HID, D), BF16),
            pltpu.VMEM((NT, 8 * CAP, 128), BF16),
            pltpu.VMEM((4, 8 * CAP, 512), BF16),
            pltpu.VMEM((8 * CAP, 128), BF16),
            pltpu.VMEM((4, 8, CAP, 512), BF16),
            pltpu.VMEM((NT, CAP, 128), BF16),
            pltpu.VMEM((2, 8 * CAP, HID), F32),
            pltpu.VMEM((8 * CAP, TOK), BF16),
            pltpu.VMEM((8 * CAP, TOK), BF16),
            pltpu.VMEM((HID, HID), BF16),
            pltpu.VMEM((2 * HID, 2 * HID), BF16),
            pltpu.VMEM((8 * CAP, HID), BF16),
            pltpu.VMEM((8 * CAP, HID), BF16),
            pltpu.VMEM((8 * CAP, HID), BF16),
            pltpu.VMEM((8 * CAP, HID), BF16),
            pltpu.VMEM((NT, 8 * CAP, 128), BF16),
            pltpu.VMEM((15872, 128), BF16),
            pltpu.VMEM((4, 8, 4, CAP, 128), BF16),
            pltpu.VMEM((4, 8, 4, CAP, 128), BF16),
            pltpu.VMEM((4, NZ, CAP, 128), BF16),
            pltpu.VMEM((3, NZ, CAP, 128), BF16),
            pltpu.VMEM((NZ - 1, CAP, 128), BF16),
            pltpu.VMEM((8 * CAP, 128), BF16),
            dma((4,)), dma((168,)), dma((2,)), dma((2,)), dma((5,)),
        ],
        compiler_params=pltpu.CompilerParams(
            collective_id=0, has_side_effects=True, vmem_limit_bytes=60 * 2**20
        ),
        cost_estimate=pl.CostEstimate(flops=10**10, bytes_accessed=2 * 10**7, transcendentals=2**18),
        name="moe_layer",
    )(routes.T, gate_num.T, tokens, gate_weight[0], up_weight[0], down_weight[0])


def solution(mesh):
    placed = (
        P("expert", None),
        P("expert", None),
        P("expert", None),
        P("expert", None, "tensor"),
        P("expert", None, "tensor"),
        P("expert", "tensor", None),
    )
    return jax.shard_map(
        shards, mesh=mesh, in_specs=placed, out_specs=P("expert", "tensor"), check_vma=False
    )
```

time: 419 us -> 103 us (0.25)
  waiting for transfers between devices: 260 us -> 0 us
  Pallas kernels: 0 us -> 101 us
  blocking collectives: 93.4 us -> 0 us
  matrix products: 20.3 us -> 0 us
  starting transfers between devices: 15.3 us -> 0 us
  between operations: 13.5 us -> 0.01 us
  other arithmetic: 10.9 us -> 0 us
    reduce_scatter x1 -> x0, waiting for transfers between devices: 224 us -> none  [shards(): lax.psum_scatter(partial_value.astype(jnp.bfloat16), 'tensor', scatter_di...]
    pallas_call x0 -> x1, Pallas kernels: none -> 101 us  [shards(): pl.pallas_call(kernel, out_shape=jax.ShapeDtypeStruct((TOK, 192), BF16),...]
    all_to_all x2 -> x0, blocking collectives: 93.4 us -> none  [the longest x1 78.1 us: shards(): lax.all_to_all(outgoing, 'expert', split_axis=0, concat_axis=0, tiled=True)]
    ppermute x5 -> x0, waiting for transfers between devices: 35.6 us -> none  [partner_2(): lax.ppermute(value, axis, [(i, i ^ 1 << apart) for i in range(lax.axis_si...]
    dot_general x5 -> x0, matrix products: 20.3 us -> none  [the longest x1 6.82 us: shards(): jnp.dot(hidden, local_sign, preferred_element_type=jnp.float32)]
    ppermute x5 -> x0, starting transfers between devices: 15.3 us -> none  [partner_2(): lax.ppermute(value, axis, [(i, i ^ 1 << apart) for i in range(lax.axis_si...]
    convert_element_type x5 -> x0, other arithmetic: 8 us -> none  [the longest x4 8 us: shards(): transformed.astype(jnp.bfloat16)]
  transfers between devices with their start and end apart: 6 -> 0, of which waited for: 6 -> 0; matrix products, arithmetic and copies ran while one was open for 0% -> 0% of each run, Pallas kernels for 0% -> 0%
where the time goes in v2:
time: 103 us
  Pallas kernels  101 us (98%)
  local copies, waits for them, and re-layouts  1.56 us (2%)
    pallas_call x1, Pallas kernels, shards(): pl.pallas_call(kernel, out_shape=jax.ShapeDtypeStruct((TOK, 192), BF16),...  101 us

profile of v2, /device:TPU:1, one launch (start us, length us, event | category | flops | bytes accessed | tf_op | source)
XLA Modules:
  0.0 102.6 jit_solution(13354441501793805404)
XLA Ops:
  0.0 101.0 %moe_layer.1 = bf16[128,192]{1,0:T(8,128)(2,1)} custom-call(s32[2,128]{1,0:T(2,128)} %bitcast.8, s32[2,128]{1,0:T(2,128)} %bitcast.9, bf16[128,6144]{1,0:T(8,128)(2,1)} %tok_ref.1, bf16[6144,256]{1,0:T(8,128)(2,1)} %bitcast.5, bf16[6144,256]{1,0:T(8,128)(2,1)} %bitcast.6, bf16[256,6144]{1,0:T(8,128)(2,1)} %bitcast.7), custom_call_target="tpu_custom_call" | custom-call | flops 10000000000 | bytes 20000000 | tf_op jit(solution)/shard_map/moe_layer/pallas_call | solution.py:490
  101.0 1.6 %copy.7 = bf16[128,192]{0,1:T(8,128)(2,1)} copy(bf16[128,192]{1,0:T(8,128)(2,1)} %moe_layer.1) | data formatting | bytes 98304 | tf_op jit(solution)/shard_map/moe_layer/pallas_call | solution.py:490

commit v3 on v2

--- a/solution.py
+++ b/solution.py
@@ -14,9 +14,9 @@
 BF16, F32 = jnp.bfloat16, jnp.float32
 
 PEERS = tuple((dx, dc) for dx in (0, 2, 1, 3) for dc in (0, 1))
-GATHER = ((128, 224), (352, 160))
-REDUCE = ((0, 288), (288, 224))
-LATENCY, B_PAUSE = 2.2, 6.0
+GATHER = ((128, 256), (384, 128))
+REDUCE = ((0, 256), (256, 256))
+LATENCY, B_PAUSE = 1.6, 6.0
 
 
 class Node:
@@ -192,17 +192,12 @@
         columns = pl.ds(pl.multiple_of(own_t * 128, 128), 128)
         sliced[...] = jnp.dot(pick[...], tok_ref[:, columns], preferred_element_type=F32).astype(BF16)
 
-    def chunk_rows(low, high):
-        for k in range(4):
-            columns = tok_ref[:, YZ_COLS + 512 * k : YZ_COLS + 512 * (k + 1)]
-            area = slice(low * CAP, high * CAP)
-            rows = jnp.dot(pick[area, :], columns, preferred_element_type=F32).astype(BF16)
-            for number in range(low, high):
-                piece = rows[(number - low) * CAP : (number - low + 1) * CAP]
-                if number == 0:
-                    wide[k, 0:CAP, :] = piece
-                else:
-                    chunked[k, number] = piece
+    def chunk_rows(k):
+        columns = tok_ref[:, YZ_COLS + 512 * k : YZ_COLS + 512 * (k + 1)]
+        rows = jnp.dot(pick[...], columns, preferred_element_type=F32).astype(BF16)
+        wide[k, 0:CAP, :] = rows[0:CAP]
+        for number in range(1, 8):
+            chunked[k, number] = rows[number * CAP : (number + 1) * CAP]
 
     def near_rows():
         for t in range(NT):
@@ -213,8 +208,8 @@
 
     tables()
     slice_rows()
-    chunk_rows(0, 8)
-    near_task = task(near_rows, [], 0.5)
+    chunk_tasks = [task(lambda k=k: chunk_rows(k), [], 0.25) for k in range(4)]
+    near_task = task(near_rows, chunk_tasks, 0.5)
 
     slices, chunk_nodes = [], []
     for number in (2, 3, 4, 5, 6, 7):
@@ -230,7 +225,7 @@
                 peer_way(number), 65536,
                 lambda k=k, number=number: chunked.at[k, number],
                 lambda k=k, number=number: wide.at[k, pl.ds(lands(*PEERS[number]) * CAP, CAP)],
-                bundle=("chunk", k),
+                [chunk_tasks[k]] + (chunk_nodes[k - 2] if k > 1 else []), bundle=("chunk", k),
             )
             for number in (2, 3, 4, 5, 6, 7, 1)
         ])
@@ -292,16 +287,16 @@
         return pl.ds(pl.multiple_of(t * 16, 16), 16)
 
     def start_all(src, dst, turn):
-        def start(k, carry):
-            other = slot(lax.div(k, NZ), lax.rem(k, NZ))
+        for dy, dz in sorted(
+            [(dy, dz) for dy in range(NY) for dz in range(NZ) if dy or dz],
+            key=lambda d: -min(d[0], NY - d[0]) - min(d[1], NZ - d[1]),
+        ):
+            other = slot(dy, dz)
             pltpu.make_async_remote_copy(
                 src_ref=src.at[piece(other)], dst_ref=dst.at[piece(own_t)],
                 send_sem=b_send.at[turn], recv_sem=b_recv.at[turn],
                 device_id=(own_e, other), device_id_type=MESH,
             ).start()
-            return carry
-
-        lax.fori_loop(1, NT, start, 0)
         dst[piece(own_t), :] = src[piece(own_t), :]
 
     def all_of(ref, turn):
@@ -317,7 +312,7 @@
         back_rows[...] = (values * (1.0 / math.sqrt(NT * HID))).astype(BF16)
         start_all(back_rows, turned, 1)
 
-    dots = [task(lambda k=k: chunk_dot(k), chunk_nodes[k] + [wide_weights], 0.5) for k in range(4)]
+    dots = [task(lambda k=k: chunk_dot(k), chunk_nodes[k] + [chunk_tasks[k], wide_weights], 0.5) for k in range(4)]
     for group in (0, 1, 3, 2):
         dots.append(task(
             lambda group=group: group_dot(group),
@@ -357,17 +352,15 @@
         ]
 
     def blended(rows):
-        return lax.dot_general(blend[...], rows, (((0,), (0,)), ((), ())), preferred_element_type=F32)
+        return lax.dot_general(rows, blend[...], (((0,), (0,)), ((), ())), preferred_element_type=F32)
 
     packed = {}
     for group in (2, 1, 3, 0):
         def pack(group=group):
-            lane = iotas(CAP, 128)[1]
             for q in range(4):
-                sums = blended(cross_in[group, 0:8, q].reshape(8 * CAP, 128))
-                top, low = sums[0:CAP], sums[CAP:TOK]
-                over[group, 2 * q] = jnp.where(lane < 64, top, pltpu.roll(low, 64, 1)).astype(BF16)
-                over[group, 2 * q + 1] = jnp.where(lane < 64, pltpu.roll(top, 64, 1), low).astype(BF16)
+                sums = blended(cross_in[group, 0:8, q].reshape(8 * CAP, 128)).astype(BF16)
+                over[group, 2 * q] = sums[0:CAP]
+                over[group, 2 * q + 1] = sums[CAP : 2 * CAP]
 
         packed[group] = task(pack, cross_nodes[group] + [group_task[group]], 0.4)
 
@@ -397,7 +390,7 @@
 
     total, base = 0, len(nodes)
     reduction = tree(*REDUCE)
-    roots = [group_task[0]]
+    roots = {False: [group_task[0]], True: [group_task[0]]}
     for number, ((dy, dz), (sy, sz), (low, count), deps) in enumerate(reduction):
         def src(sy=sy, sz=sz, dy=dy, dz=dz, low=low, count=count):
             return part.at[slot(sy - dy, sz - dz), pl.ds(low, count)]
@@ -411,14 +404,14 @@
 
         children = [base + n for n, other in enumerate(reduction) if number in other[3]]
         if not deps:
-            roots.append(base + number)
+            roots[low >= REDUCE[1][0]].append(base + number)
         needs = [group_task[(sy - dy) % 4], group_task[sy % 4]]
         message((0, -dy, -dz), count * 256, src, dst, children + needs, act, count / 4000, sender=3)
         total += count
     lasts = [
         message(
             peer_way(n), 16384, lambda n=n: part.at[own_t, pl.ds(n * CAP, CAP)],
-            lambda n=n: last_in.at[pl.ds(lands(*PEERS[n]) * CAP, CAP)], roots, bundle="last", sender=2,
+            lambda n=n: last_in.at[pl.ds(lands(*PEERS[n]) * CAP, CAP)], roots[n > 3], bundle="last", sender=2,
         )
         for n in (2, 3, 4, 5, 6, 7, 1)
     ]
@@ -426,17 +419,12 @@
     def store():
         last_in[0:CAP, :] = part[own_t, 0:CAP, :]
         summed = blended(last_in[...])
-        rolled = pltpu.roll(summed, 64, 1)
+        odd = lax.rem(own_t, 2)
+        out_ref[pl.ds(pl.multiple_of(odd * CAP, CAP), TOK), :] = summed.astype(BF16)
         extra = over[0, z].astype(F32)
         for index in range(NZ - 1):
             extra = extra + over_last[index].astype(F32)
-        extra = jnp.concatenate([extra, pltpu.roll(extra, 64, 1)], axis=0)
-        odd = lax.rem(own_t, 2) == 1
-        lane = iotas(TOK, 128)[1]
-        left = jnp.where(odd, jnp.where(lane < 64, extra, rolled), summed)
-        right = jnp.where(odd, rolled, extra)
-        out_ref[:, 0:128] = left.astype(BF16)
-        out_ref[:, 128:192] = right[:, 0:64].astype(BF16)
+        out_ref[pl.ds(pl.multiple_of((1 - odd) * TOK, CAP), CAP), :] = extra.astype(BF16)
 
     task(store, lasts + ends, 0.2)
 
@@ -489,7 +477,7 @@
     dma = pltpu.SemaphoreType.DMA
     return pl.pallas_call(
         kernel,
-        out_shape=jax.ShapeDtypeStruct((TOK, 192), BF16),
+        out_shape=jax.ShapeDtypeStruct((192, TOK), BF16),
         in_specs=[vmem, vmem, vmem, anywhere, anywhere, anywhere],
         out_specs=vmem,
         scratch_shapes=[
@@ -524,7 +512,7 @@
         ),
         cost_estimate=pl.CostEstimate(flops=10**10, bytes_accessed=2 * 10**7, transcendentals=2**18),
         name="moe_layer",
-    )(routes.T, gate_num.T, tokens, gate_weight[0], up_weight[0], down_weight[0])
+    )(routes.T, gate_num.T, tokens, gate_weight[0], up_weight[0], down_weight[0]).T
 
 
 def solution(mesh):

time: 103 us -> 99 us (0.961)
  Pallas kernels: 101 us -> 97.1 us
    pallas_call x1, Pallas kernels: 101 us -> 97.1 us  [shards(): pl.pallas_call(kernel, out_shape=jax.ShapeDtypeStruct((192, TOK), BF16),...]
    pallas_call x1 -> x0, local copies, waits for them, and re-layouts: 1.56 us -> none  [shards(): pl.pallas_call(kernel, out_shape=jax.ShapeDtypeStruct((TOK, 192), BF16),...]
    unnamed x0 -> x1, local copies, waits for them, and re-layouts: none -> 1.42 us
where the time goes in v3:
time: 99 us; the launch traced here: 98.5 us
  Pallas kernels  97.1 us (98%)
  local copies, waits for them, and re-layouts  1.42 us (1%)
    pallas_call x1, Pallas kernels, shards(): pl.pallas_call(kernel, out_shape=jax.ShapeDtypeStruct((192, TOK), BF16),...  97.1 us

profile of v3, /device:TPU:1, one launch (start us, length us, event | category | flops | bytes accessed | tf_op | source)
XLA Modules:
  0.0 98.5 jit_solution(3819545530531113629)
XLA Ops:
  0.0 97.1 %moe_layer.1 = bf16[192,128]{1,0:T(8,128)(2,1)} custom-call(s32[2,128]{1,0:T(2,128)} %bitcast.10, s32[2,128]{1,0:T(2,128)} %bitcast.11, bf16[128,6144]{1,0:T(8,128)(2,1)} %tok_ref.1, bf16[6144,256]{1,0:T(8,128)(2,1)} %bitcast.7, bf16[6144,256]{1,0:T(8,128)(2,1)} %bitcast.8, bf16[256,6144]{1,0:T(8,128)(2,1)} %bitcast.9), custom_call_target="tpu_custom_call" | custom-call | flops 10000000000 | bytes 20000000 | tf_op jit(solution)/shard_map/moe_layer/pallas_call | solution.py:478
  97.1 1.4 %copy.8 = bf16[128,192]{0,1:T(8,128)(2,1)} copy(bf16[128,192]{0,1:T(8,128)(2,1)} %bitcast.6) | data formatting | bytes 98304

commit v4 on v3

--- a/solution.py
+++ b/solution.py
@@ -20,9 +20,10 @@
 
 
 class Node:
-    def __init__(self, deps, cost, act=None, way=None, size=0, src=None, dst=None, pause=0.0, bundle=None, sender=None):
+    def __init__(self, deps, cost, act=None, way=None, size=0, src=None, dst=None, pause=0.0, bundle=None, sender=None, mark=None):
         self.deps, self.cost, self.act, self.pause = list(deps), cost, act, pause
         self.way, self.size, self.src, self.dst, self.bundle, self.sender = way, size, src, dst, bundle, sender
+        self.mark = mark or bundle
 
 
 def steps_of(nodes):
@@ -144,8 +145,8 @@
 
     nodes = []
 
-    def message(way, size, src, dst, deps=(), act=None, cost=0.04, bundle=None, sender=0):
-        nodes.append(Node(deps, cost, act, way, size, src, dst, bundle=bundle, sender=sender))
+    def message(way, size, src, dst, deps=(), act=None, cost=0.04, bundle=None, sender=0, mark=None):
+        nodes.append(Node(deps, cost, act, way, size, src, dst, bundle=bundle, sender=sender, mark=mark))
         return len(nodes) - 1
 
     def task(act, deps, cost, pause=0.0):
@@ -234,11 +235,14 @@
     )
     group_nodes = [list(slices), [], [], []]
     base = len(nodes)
-    for (dy, dz), (sy, sz), (low, count), deps in tree(*GATHER):
+    for index, ((dy, dz), (sy, sz), (low, count), deps) in enumerate(tree(*GATHER)):
         def ref(sy=sy, sz=sz, low=low, count=count):
             return tiles.at[slot(sy, sz), pl.ds(low, count)]
 
-        number = message((0, dy, dz), count * 256, ref, ref, [base + d for d in deps] if deps else slices, sender=1)
+        number = message(
+            (0, dy, dz), count * 256, ref, ref, [base + d for d in deps] if deps else slices,
+            sender=1, mark=("tree", index),
+        )
         group_nodes[(sy - dy) % 4].append(number)
 
     def fold_signs():
@@ -278,26 +282,30 @@
     def chunk_dot(k):
         accumulate(wide[k], YZ_COLS + 512 * k, 512)
 
+    def block(group):
+        return pl.ds(pl.multiple_of(lax.rem(y + group, NY) * TOK, TOK), TOK)
+
     def hide():
-        gate, up = acc[0], acc[1]
-        hidden = (gate / (1.0 + jnp.exp(-gate)) * up).astype(BF16)
-        sent_rows[...] = jnp.dot(hidden, fold[...], preferred_element_type=F32).astype(BF16)
+        for group in (2, 1, 3, 0):
+            gate, up = acc[0, block(group), :], acc[1, block(group), :]
+            hidden = (gate / (1.0 + jnp.exp(-gate)) * up).astype(BF16)
+            sent_rows[block(group), :] = jnp.dot(hidden, fold[...], preferred_element_type=F32).astype(BF16)
+            start_block(sent_rows, got_rows, 0, group)
 
     def piece(t):
         return pl.ds(pl.multiple_of(t * 16, 16), 16)
 
-    def start_all(src, dst, turn):
-        for dy, dz in sorted(
-            [(dy, dz) for dy in range(NY) for dz in range(NZ) if dy or dz],
-            key=lambda d: -min(d[0], NY - d[0]) - min(d[1], NZ - d[1]),
-        ):
-            other = slot(dy, dz)
-            pltpu.make_async_remote_copy(
-                src_ref=src.at[piece(other)], dst_ref=dst.at[piece(own_t)],
-                send_sem=b_send.at[turn], recv_sem=b_recv.at[turn],
-                device_id=(own_e, other), device_id_type=MESH,
-            ).start()
-        dst[piece(own_t), :] = src[piece(own_t), :]
+    def start_block(src, dst, turn, group):
+        for dz in (4, 3, -3, 2, -2, 1, -1, 0):
+            other = slot(group, dz)
+            if group or dz:
+                pltpu.make_async_remote_copy(
+                    src_ref=src.at[piece(other)], dst_ref=dst.at[piece(own_t)],
+                    send_sem=b_send.at[turn], recv_sem=b_recv.at[turn],
+                    device_id=(own_e, other), device_id_type=MESH,
+                ).start()
+            else:
+                dst[piece(own_t), :] = src[piece(own_t), :]
 
     def all_of(ref, turn):
         area = ref.at[pl.ds(0, (NT - 1) * 16)]
@@ -308,9 +316,10 @@
 
     def rotate():
         all_of(got_rows, 0).wait_recv()
-        values = jnp.dot(mix[...], got_rows[...], preferred_element_type=F32)
-        back_rows[...] = (values * (1.0 / math.sqrt(NT * HID))).astype(BF16)
-        start_all(back_rows, turned, 1)
+        for group in (2, 1, 3, 0):
+            values = jnp.dot(mix[block(group), :], got_rows[...], preferred_element_type=F32)
+            back_rows[block(group), :] = (values * (1.0 / math.sqrt(NT * HID))).astype(BF16)
+            start_block(back_rows, turned, 1, group)
 
     dots = [task(lambda k=k: chunk_dot(k), chunk_nodes[k] + [chunk_tasks[k], wide_weights], 0.5) for k in range(4)]
     for group in (0, 1, 3, 2):
@@ -318,8 +327,7 @@
             lambda group=group: group_dot(group),
             group_nodes[group] + [tile_weights, near_node, near_task], 0.9,
         ))
-    hidden_task = task(hide, dots + [fold_task], 1.0)
-    gone = task(lambda: start_all(sent_rows, got_rows, 0), [hidden_task], 1.0)
+    gone = task(hide, dots + [fold_task], 1.6)
     back = task(rotate, [gone] + mix_tasks, 1.5, B_PAUSE)
     come = task(lambda: all_of(turned, 1).wait_recv(), [back], 0.1, B_PAUSE)
 
@@ -406,7 +414,7 @@
         if not deps:
             roots[low >= REDUCE[1][0]].append(base + number)
         needs = [group_task[(sy - dy) % 4], group_task[sy % 4]]
-        message((0, -dy, -dz), count * 256, src, dst, children + needs, act, count / 4000, sender=3)
+        message((0, -dy, -dz), count * 256, src, dst, children + needs, act, count / 4000, sender=3, mark=("tree", number))
         total += count
     lasts = [
         message(
@@ -428,18 +436,14 @@
 
     task(store, lasts + ends, 0.2)
 
-    marks = []
-    for number, node in enumerate(nodes):
-        if node.way:
-            key = node.bundle or number
-            if key not in marks:
-                marks.append(key)
+    marks = sorted({str(node.mark) for node in nodes if node.way and node.mark})
+    marks += [str(number) for number, node in enumerate(nodes) if node.way and not node.mark]
 
     def copy_of(number, src=None, dst=None):
         node = nodes[number]
         return pltpu.make_async_remote_copy(
             src_ref=src or node.src(), dst_ref=dst or node.dst(),
-            send_sem=sends.at[node.sender], recv_sem=recvs.at[marks.index(node.bundle or number)],
+            send_sem=sends.at[node.sender], recv_sem=recvs.at[marks.index(str(node.mark or number))],
             device_id=device(*node.way), device_id_type=MESH,
         )
 
@@ -505,7 +509,7 @@
             pltpu.VMEM((3, NZ, CAP, 128), BF16),
             pltpu.VMEM((NZ - 1, CAP, 128), BF16),
             pltpu.VMEM((8 * CAP, 128), BF16),
-            dma((4,)), dma((168,)), dma((2,)), dma((2,)), dma((5,)),
+            dma((4,)), dma((91,)), dma((2,)), dma((2,)), dma((5,)),
         ],
         compiler_params=pltpu.CompilerParams(
             collective_id=0, has_side_effects=True, vmem_limit_bytes=60 * 2**20

time: 99 us -> 96.7 us (0.977)
  Pallas kernels: 97.1 us -> 95.1 us
    pallas_call x1, Pallas kernels: 97.1 us -> 95.1 us  [shards(): pl.pallas_call(kernel, out_shape=jax.ShapeDtypeStruct((192, TOK), BF16),...]
where the time goes in v4:
time: 96.7 us; the launch traced here: 96.5 us
  Pallas kernels  95.1 us (98%)
  local copies, waits for them, and re-layouts  1.42 us (1%)
    pallas_call x1, Pallas kernels, shards(): pl.pallas_call(kernel, out_shape=jax.ShapeDtypeStruct((192, TOK), BF16),...  95.1 us

profile of v4, /device:TPU:1, one launch (start us, length us, event | category | flops | bytes accessed | tf_op | source)
XLA Modules:
  0.0 96.5 jit_solution(7984179080209668970)
XLA Ops:
  0.0 95.1 %moe_layer.1 = bf16[192,128]{1,0:T(8,128)(2,1)} custom-call(s32[2,128]{1,0:T(2,128)} %bitcast.10, s32[2,128]{1,0:T(2,128)} %bitcast.11, bf16[128,6144]{1,0:T(8,128)(2,1)} %tok_ref.1, bf16[6144,256]{1,0:T(8,128)(2,1)} %bitcast.7, bf16[6144,256]{1,0:T(8,128)(2,1)} %bitcast.8, bf16[256,6144]{1,0:T(8,128)(2,1)} %bitcast.9), custom_call_target="tpu_custom_call" | custom-call | flops 10000000000 | bytes 20000000 | tf_op jit(solution)/shard_map/moe_layer/pallas_call | solution.py:482
  95.1 1.4 %copy.8 = bf16[128,192]{0,1:T(8,128)(2,1)} copy(bf16[128,192]{0,1:T(8,128)(2,1)} %bitcast.6) | data formatting | bytes 98304

commit v5 on v4

--- a/solution.py
+++ b/solution.py
@@ -124,11 +124,10 @@
     for dx, dc in PEERS[1:]:
         pl.semaphore_signal(barrier, inc=1, device_id=device(dx, 0, 0, dc), device_id_type=MESH)
 
-    def greet(k, carry):
-        pl.semaphore_signal(barrier, inc=1, device_id=device(0, lax.div(k, NZ), lax.rem(k, NZ)), device_id_type=MESH)
-        return carry
-
-    lax.fori_loop(1, NT, greet, 0)
+    for dz in (4, 3, -3, 2, -2, 1, -1, 0):
+        for dy in (2, 1, -1, 0):
+            if dy or dz:
+                pl.semaphore_signal(barrier, inc=1, device_id=device(0, dy, dz), device_id_type=MESH)
 
     areas = (pl.ds(YZ_COLS, D - YZ_COLS), pl.ds(0, YZ_COLS))
 

time: 96.7 us -> 97 us (level)
  no operation moved by 1% of the time
where the time goes in v5:
time: 97 us; the launch traced here: 96.9 us
  Pallas kernels  95.4 us (98%)
  local copies, waits for them, and re-layouts  1.42 us (1%)
    pallas_call x1, Pallas kernels, shards(): pl.pallas_call(kernel, out_shape=jax.ShapeDtypeStruct((192, TOK), BF16),...  95.4 us

profile of v5, /device:TPU:1, one launch (start us, length us, event | category | flops | bytes accessed | tf_op | source)
XLA Modules:
  0.0 96.9 jit_solution(2525497560843974875)
XLA Ops:
  0.0 95.4 %moe_layer.1 = bf16[192,128]{1,0:T(8,128)(2,1)} custom-call(s32[2,128]{1,0:T(2,128)} %bitcast.10, s32[2,128]{1,0:T(2,128)} %bitcast.11, bf16[128,6144]{1,0:T(8,128)(2,1)} %tok_ref.1, bf16[6144,256]{1,0:T(8,128)(2,1)} %bitcast.7, bf16[6144,256]{1,0:T(8,128)(2,1)} %bitcast.8, bf16[256,6144]{1,0:T(8,128)(2,1)} %bitcast.9), custom_call_target="tpu_custom_call" | custom-call | flops 10000000000 | bytes 20000000 | tf_op jit(solution)/shard_map/moe_layer/pallas_call | solution.py:481
  95.5 1.4 %copy.8 = bf16[128,192]{0,1:T(8,128)(2,1)} copy(bf16[128,192]{0,1:T(8,128)(2,1)} %bitcast.6) | data formatting | bytes 98304
